TPU v7x, 32 devices: a whole 2x2x4 slice. The times are simulated.
32 devices in a mesh: grp: 2 (over y), rows: 8 (over z, x), mod: 2 (over core).
Axes of the slice: x: 2, y: 2, z: 4, core: 2. Of those that a mesh axis runs over, the one named last changes fastest.
Arguments:
- queries: bfloat16 [16, 8, 2304], P(('grp', 'rows'), 'mod'), parts along dimension 0, may hold values from -6 to 6
- train_grads: bfloat16 [2048, 8, 2304], P(('grp', 'rows'), 'mod'), parts along dimension 0, may hold values from -6 to 6
- factors: float32 [8, 2, 48, 48], P('mod'), may hold values from -4 to 4, as said below
Outputs:
- scores: float32 [16, 1024], P(('grp', 'mod'), 'rows'), parts along dimension 0
There are 2 independent parts, one for each index of `grp`. A program takes and returns all parts, laid end to end along the dimension named above; an argument that names none is the same for every part. Nothing has to cross between parts.
Inputs may be any that keep to these rules, and one draw needn't show every extreme that they name: `factors`: each factor is a 48 x 48 matrix with a positive diagonal and full rank.
All inputs are finite; a program needn't handle non-finite values.
Results may differ from a plain program's by a relative error of at most 0.0029.
Values may be sent and summed in bfloat16 or wider, within the bound.
A program may use at most 64 MiB of HBM per device.

v0:
```python
import jax
import jax.numpy as jnp
from jax import lax
from jax.sharding import PartitionSpec as P

MODULES = 8
PROJ = 48
COORDS = 2304


def precondition(grads_in, factors):
    count = grads_in.shape[0]
    local_modules = grads_in.shape[1]
    grads = grads_in.astype(jnp.float32).reshape(count, local_modules, PROJ, PROJ)
    left_side = jnp.einsum("mab,qmbc->qmac", factors[:, 0], grads, precision=lax.Precision.HIGHEST)
    both_sides = jnp.einsum(
        "qmac,mcd->qmad", left_side, factors[:, 1], precision=lax.Precision.HIGHEST
    )
    both_sides = both_sides / jnp.sqrt(jnp.float32(MODULES * COORDS))
    return both_sides.astype(jnp.bfloat16).reshape(count, local_modules, PROJ * PROJ)


def shards(queries, train_grads, factors):
    train_count = train_grads.shape[0]
    train_flat = train_grads.reshape(train_count, -1)
    scaled_own = precondition(queries, factors)
    ready_rows = lax.all_gather(scaled_own, "rows", axis=0, tiled=True)
    flat_rows = ready_rows.reshape(ready_rows.shape[0], -1)
    partial_value = lax.dot_general(
        flat_rows, train_flat, (((1,), (1,)), ((), ())), preferred_element_type=jnp.float32
    )
    return lax.psum_scatter(partial_value, "mod", scatter_dimension=0, tiled=True)


def solution(mesh):
    in_specs = (
        P(("grp", "rows"), "mod", None),
        P(("grp", "rows"), "mod", None),
        P("mod", None, None, None),
    )
    out_specs = P(("grp", "mod"), "rows")
    return jax.shard_map(shards, mesh=mesh, in_specs=in_specs, out_specs=out_specs, check_vma=False)
```

profile of v0, /device:TPU:0, one launch (start us, length us, event | category | flops | bytes accessed | tf_op | source)
XLA Modules:
  0.0 40.9 jit_solution(16463728505834022918)
XLA Ops:
  0.0 0.0 copy-start
  0.0 0.0 copy-start.1
  0.0 1.0 %reshape.18 = bf16[4,48,48]{2,1,0:T(8,128)(2,1)S(1)} reshape(bf16[1,4,2304]{2,1,0:T(4,128)(2,1)} %param.3) | data formatting | bytes 36864 | tf_op jit(solution)/shard_map/reshape
  1.0 1.2 %convolution_bitcast_fusion = f32[4,48,48]{1,2,0:T(8,128)S(1)} fusion(bf16[4,48,48]{2,1,0:T(8,128)(2,1)S(1)} %reshape.18, f32[4,2,48,48]{3,2,1,0:T(8,128)} %param.5), kind=kOutput, calls=%fused_computation.3 | convolution fusion | flops 5308416 | bytes 153600 | tf_op jit(solution)/shard_map/mab,qmbc->qmac/dot_general | solution.py:15
  2.1 1.2 %fusion.3 = bf16[1,4,48,48]{3,2,1,0:T(8,128)(2,1)S(1)} fusion(f32[4,48,48]{1,2,0:T(8,128)S(1)} %convolution_bitcast_fusion, f32[4,2,48,48]{3,2,1,0:T(8,128)} %param.5), kind=kOutput, calls=%fused_computation.5 | convolution fusion | flops 5326848 | bytes 153600 | tf_op jit(solution)/shard_map/qmac,mcd->qmad/dot_general | solution.py:16
  3.4 0.1 reshape.20
  3.5 32.3 %all_gather.3 = bf16[8,4,2304]{2,1,0:T(4,128)(2,1)S(1)} all-gather(bf16[1,4,2304]{2,1,0:T(4,128)(2,1)S(1)} %reshape.20), channel_id=1, replica_groups=mesh['grp'=2,'rows'=8,'mod'=2] {'rows'}, dimensions={0}, use_global_device_ids=true | all-gather | bytes 165888 | tf_op jit(solution)/shard_map/all_gather | solution.py:27
  35.9 0.0 copy-done
  35.9 0.7 %fusion.4 = f32[8,128]{1,0:T(8,128)S(1)} fusion(bf16[128,4,2304]{2,1,0:T(4,128)(2,1)S(1)} %copy-done, bf16[8,4,2304]{2,1,0:T(4,128)(2,1)S(1)} %all_gather.3), kind=kOutput, calls=%fused_computation.6 | convolution fusion | flops 18874368 | bytes 2510848 | tf_op jit(solution)/shard_map/dot_general | solution.py:29
  36.6 2.5 %all-reduce = f32[8,128]{1,0:T(8,128)S(1)} all-reduce(f32[8,128]{1,0:T(8,128)S(1)} %fusion.4), channel_id=2, replica_groups=mesh['grp'=2,'rows'=8,'mod'=2] {'mod'}, use_global_device_ids=true, to_apply=%region_0.0.clone | all-reduce | flops 1024 | bytes 8192
  39.0 0.0 copy-done.1
  39.0 0.6 %dynamic-slice = u32[1]{0:T(128)} dynamic-slice(u32[32]{0:T(128)S(1)} %copy-done.1, u32[]{:T(128)S(6)} %add.3), dynamic_slice_sizes={1} | dynamic-slice | bytes 12
  40.3 0.6 %constant_dynamic-slice_fusion = f32[4,128]{1,0:T(4,128)} fusion(f32[8,128]{1,0:T(8,128)S(1)} %all-reduce, u32[]{:T(128)S(6)} %multiply.5), kind=kLoop, calls=%fused_computation.12 | loop fusion | bytes 4100
Async XLA Ops:
  0.0 35.9 %copy-start = (bf16[128,4,2304]{2,1,0:T(4,128)(2,1)S(1)}, bf16[128,4,2304]{2,1,0:T(4,128)(2,1)}, u32[]{:S(2)}) copy-start(bf16[128,4,2304]{2,1,0:T(4,128)(2,1)} %param.4) | copy-start | bytes 7077892
  0.0 39.0 %copy-start.1 = (u32[32]{0:T(128)S(1)}, u32[32]{0:T(128)}, u32[]{:S(2)}) copy-start(u32[32]{0:T(128)} %constant.6) | copy-start | bytes 388
where the time goes:
time: 41.1 us; the launch traced here: 40.9 us
  blocking collectives  34.8 us (85%)
  matrix products  3.1 us (8%)
  local copies, waits for them, and re-layouts  2.27 us (6%)
  between operations  0.68 us (2%)
    all_gather x1, blocking collectives, shards(): ready_rows = lax.all_gather(scaled_own, 'rows', axis=0, tiled=True)  32.3 us
    unnamed x1, blocking collectives  2.46 us
    dot_general x1, matrix products, precondition(): jnp.einsum('qmac,mcd->qmad', left_side, factors[:, 1], precision=lax.Prec...  1.24 us
    unnamed x6, local copies, waits for them, and re-layouts  1.18 us
    dot_general x1, matrix products, precondition(): jnp.einsum('mab,qmbc->qmac', factors[:, 0], grads, precision=lax.Precisio...  1.15 us
    reshape x1, local copies, waits for them, and re-layouts  0.98 us

commit v1 on v0

v1 whole, which is shorter than its diff:
```python
import functools
import math

import jax
import jax.numpy as jnp
from jax import lax
from jax.experimental import pallas as pl
from jax.experimental.pallas import tpu as pltpu
from jax.sharding import PartitionSpec as P

HIGHEST = lax.Precision.HIGHEST
LANES = 128
GROUP = 8


def iota(shape, dim):
    return lax.broadcasted_iota(jnp.int32, shape, dim)


def zero_one(mask):
    return jnp.where(mask, 1.0, 0.0).astype(jnp.bfloat16)


def dot(a, b, contract, precision=None):
    return lax.dot_general(
        a, b, ((contract[:1], contract[1:]), ((), ())), precision=precision, preferred_element_type=jnp.float32
    )


def precondition(query, factors, scale, modules, side):
    chunks = side // GROUP
    width = GROUP * side
    rows = modules * side
    flat = jnp.concatenate([query[:, c * width : (c + 1) * width] for c in range(chunks)], axis=0)
    spread = zero_one(
        iota((rows, chunks * modules), 1)
        == (iota((rows, chunks * modules), 0) % side) // GROUP * modules + iota((rows, chunks * modules), 0) // side
    )
    keep = iota((rows, width), 0) % GROUP == iota((rows, width), 1) // side
    fold = zero_one(iota((width, side), 0) % side == iota((width, side), 1))
    matrices = dot(spread, flat.astype(jnp.bfloat16), (1, 0))
    matrices = jnp.where(keep, matrices, 0.0).astype(jnp.bfloat16)
    matrices = dot(matrices, fold, (1, 0))
    outs = []
    for m in range(modules):
        left = dot(factors[m, 0], matrices[m * side : (m + 1) * side], (1, 0), HIGHEST)
        outs.append(dot(left, factors[m, 1], (1, 0), HIGHEST))
    both = (jnp.concatenate(outs, axis=0) / scale).astype(jnp.bfloat16)
    wide = dot(both, fold, (1, 1))
    wide = jnp.where(keep, wide, 0.0).astype(jnp.bfloat16)
    return dot(spread, wide, (0, 0))


def kernel(
    rows_n, grp_scale, q_hbm, t_hbm, f_hbm, out_ref,
    q_v, f_v, t_v, own, held, part, other,
    in_sem, t_sem, send_sem, recv_sem, ex_sem,
):
    modules, coords = q_hbm.shape[1:]
    side = f_hbm.shape[-1]
    tiles = coords // LANES
    train = t_hbm.shape[0]
    me = lax.axis_index("rows")
    core = lax.axis_index("mod")

    q_copy = pltpu.make_async_copy(q_hbm, q_v, in_sem.at[0])
    f_copy = pltpu.make_async_copy(f_hbm, f_v, in_sem.at[1])
    q_copy.start()
    f_copy.start()

    barrier = pltpu.get_barrier_semaphore()
    for step in range(1, rows_n):
        pl.semaphore_signal(barrier, inc=1, device_id={"rows": lax.rem(me + step, rows_n)})
    pl.semaphore_signal(barrier, inc=1, device_id={"mod": 1 - core})

    t_copies = [
        pltpu.make_async_copy(t_hbm.at[:, :, pl.ds(j * LANES, LANES)], t_v.at[j], t_sem.at[j]) for j in range(tiles)
    ]
    for copy in t_copies:
        copy.start()

    q_copy.wait()
    f_copy.wait()
    scaled = precondition(q_v[0].astype(jnp.float32), f_v, grp_scale, modules, side)
    per = GROUP * side // LANES
    for j in range(tiles):
        c, t = divmod(j, per)
        piece = scaled[c * modules : (c + 1) * modules, t * LANES : (t + 1) * LANES].astype(jnp.bfloat16)
        own[j] = piece

    pl.semaphore_wait(barrier, rows_n)

    def push(step):
        return pltpu.make_async_remote_copy(
            src_ref=own,
            dst_ref=held.at[me],
            send_sem=send_sem.at[step],
            recv_sem=recv_sem.at[step],
            device_id={"rows": lax.rem(me + step, rows_n)},
        )

    def arrival(step):
        source = lax.rem(me + rows_n - step, rows_n)
        return pltpu.make_async_remote_copy(
            src_ref=own,
            dst_ref=held.at[source],
            send_sem=send_sem.at[step],
            recv_sem=recv_sem.at[step],
            device_id={"rows": lax.rem(me + step, rows_n)},
        )

    for step in range(1, rows_n):
        push(step).start()
    held[me] = own[...]
    for copy in t_copies:
        copy.wait()
    for step in range(1, rows_n):
        arrival(step).wait_recv()

    total = jnp.zeros((train * modules, rows_n * modules), jnp.float32)
    for j in range(tiles):
        a = t_v[j].reshape(train * modules, LANES)
        b = held[:, j].reshape(rows_n * modules, LANES)
        total += dot(a, b, (1, 1))
    same = iota(total.shape, 0) % modules == iota(total.shape, 1) % modules
    total = jnp.where(same, total, 0.0)
    pick_n = jnp.where(iota((train * modules, train), 0) // modules == iota((train * modules, train), 1), 1.0, 0.0)
    pick_q = jnp.where(iota((rows_n, rows_n * modules), 1) // modules == iota((rows_n, rows_n * modules), 0), 1.0, 0.0)
    by_n = dot(pick_n, total, (0, 0), HIGHEST)
    scores = dot(pick_q, by_n, (1, 1), HIGHEST)
    half = rows_n // 2
    part[0] = scores[:half]
    part[1] = scores[half:]
    swap = pltpu.make_async_remote_copy(
        src_ref=part.at[1 - core],
        dst_ref=other,
        send_sem=ex_sem.at[0],
        recv_sem=ex_sem.at[1],
        device_id={"mod": 1 - core},
    )
    swap.start()
    swap.wait_recv()
    out_ref[...] = part[core] + other[...]
    swap.wait_send()
    for step in range(1, rows_n):
        push(step).wait_send()


def shards(rows_n, cores, queries, train_grads, factors):
    _, modules, coords = queries.shape
    train = train_grads.shape[0]
    side = factors.shape[-1]
    tiles = coords // LANES
    scale = math.sqrt(cores * modules * coords)
    half = rows_n // 2
    return pl.pallas_call(
        functools.partial(kernel, rows_n, scale),
        out_shape=jax.ShapeDtypeStruct((half, train), jnp.float32),
        in_specs=[pl.BlockSpec(memory_space=pl.ANY)] * 3,
        out_specs=pl.BlockSpec(memory_space=pltpu.VMEM),
        scratch_shapes=[
            pltpu.VMEM(queries.shape, jnp.bfloat16),
            pltpu.VMEM(factors.shape, jnp.float32),
            pltpu.VMEM((tiles, train, modules, LANES), jnp.bfloat16),
            pltpu.VMEM((tiles, modules, LANES), jnp.bfloat16),
            pltpu.VMEM((rows_n, tiles, modules, LANES), jnp.bfloat16),
            pltpu.VMEM((2, half, train), jnp.float32),
            pltpu.VMEM((half, train), jnp.float32),
            pltpu.SemaphoreType.DMA((2,)),
            pltpu.SemaphoreType.DMA((tiles,)),
            pltpu.SemaphoreType.DMA((rows_n,)),
            pltpu.SemaphoreType.DMA((rows_n,)),
            pltpu.SemaphoreType.DMA((2,)),
        ],
        compiler_params=pltpu.CompilerParams(
            collective_id=0, has_side_effects=True, vmem_limit_bytes=32 * 1024 * 1024
        ),
    )(queries, train_grads, factors)


def solution(mesh):
    in_specs = (
        P(("grp", "rows"), "mod", None),
        P(("grp", "rows"), "mod", None),
        P("mod", None, None, None),
    )
    out_specs = P(("grp", "mod"), "rows")
    body = functools.partial(shards, mesh.shape["rows"], mesh.shape["mod"])
    return jax.shard_map(body, mesh=mesh, in_specs=in_specs, out_specs=out_specs, check_vma=False)
```

time: 41.1 us -> 17.3 us (0.42)
  blocking collectives: 34.8 us -> 0 us
  Pallas kernels: 0 us -> 13.2 us
  matrix products: 3.1 us -> 0 us
  local copies, waits for them, and re-layouts: 2.27 us -> 3.89 us
  between operations: 0.68 us -> 0.01 us
    all_gather x1 -> x0, blocking collectives: 32.3 us -> none  [shards(): ready_rows = lax.all_gather(scaled_own, 'rows', axis=0, tiled=True)]
    pallas_call x0 -> x1, Pallas kernels: none -> 13.2 us  [shards(): pl.pallas_call(functools.partial(kernel, rows_n, scale), out_shape=jax.Sh...]
    dot_general x3 -> x0, matrix products: 3.1 us -> none  [the longest x1 1.24 us: precondition(): jnp.einsum('qmac,mcd->qmad', left_side, factors[:, 1], precision=lax.Prec...]
    unnamed x6 -> x7, local copies, waits for them, and re-layouts: 1.18 us -> 3.89 us
    unnamed x1 -> x0, blocking collectives: 2.46 us -> none
    reshape x2 -> x0, local copies, waits for them, and re-layouts: 1.09 us -> none
where the time goes in v1:
time: 17.3 us; the launch traced here: 17.1 us
  Pallas kernels  13.2 us (76%)
  local copies, waits for them, and re-layouts  3.89 us (22%)
    pallas_call x1, Pallas kernels, shards(): pl.pallas_call(functools.partial(kernel, rows_n, scale), out_shape=jax.Sh...  13.2 us
    unnamed x7, local copies, waits for them, and re-layouts  3.89 us

profile of v1, /device:TPU:0, one launch (start us, length us, event | category | flops | bytes accessed | tf_op | source)
XLA Modules:
  0.0 17.1 jit_solution(3984118478342301344)
XLA Ops:
  0.0 0.0 copy-start
  0.0 1.7 %copy-done = bf16[128,4,2304]{2,1,0:T(4,128)(2,1)S(1)} copy-done((bf16[128,4,2304]{2,1,0:T(4,128)(2,1)S(1)}, bf16[128,4,2304]{2,1,0:T(4,128)(2,1)}, u32[]{:S(2)}) %copy-start) | copy-done | bytes 2359320
  1.7 0.0 copy-start.1
  1.7 0.9 %copy-done.1 = f32[4,2,48,48]{3,2,1,0:T(8,128)S(1)} copy-done((f32[4,2,48,48]{3,2,1,0:T(8,128)S(1)}, f32[4,2,48,48]{3,2,1,0:T(8,128)}, u32[]{:S(2)}) %copy-start.1) | copy-done | bytes 73752
  2.6 0.0 copy-start.2
  2.6 0.7 %copy-done.2 = bf16[1,4,2304]{2,1,0:T(4,128)(2,1)S(1)} copy-done((bf16[1,4,2304]{2,1,0:T(4,128)(2,1)S(1)}, bf16[1,4,2304]{2,1,0:T(4,128)(2,1)}, u32[]{:S(2)}) %copy-start.2) | copy-done | bytes 18456
  3.3 13.2 %shard_map.37 = f32[4,128]{1,0:T(4,128)S(1)} custom-call(bf16[1,4,2304]{2,1,0:T(4,128)(2,1)S(1)} %copy-done.2, bf16[128,4,2304]{2,1,0:T(4,128)(2,1)S(1)} %copy-done, f32[4,2,48,48]{3,2,1,0:T(8,128)S(1)} %copy-done.1), custom_call_target="tpu_custom_call" | custom-call | tf_op jit(solution)/shard_map/pallas_call | solution.py:156
  16.5 0.6 %copy.5 = f32[4,128]{1,0:T(4,128)} copy(f32[4,128]{1,0:T(4,128)S(1)} %shard_map.37) | data formatting | bytes 4096
Async XLA Ops:
  0.0 1.7 %copy-start = (bf16[128,4,2304]{2,1,0:T(4,128)(2,1)S(1)}, bf16[128,4,2304]{2,1,0:T(4,128)(2,1)}, u32[]{:S(2)}) copy-start(bf16[128,4,2304]{2,1,0:T(4,128)(2,1)} %t_hbm.1) | copy-start | bytes 7077892
  1.7 0.9 %copy-start.1 = (f32[4,2,48,48]{3,2,1,0:T(8,128)S(1)}, f32[4,2,48,48]{3,2,1,0:T(8,128)}, u32[]{:S(2)}) copy-start(f32[4,2,48,48]{3,2,1,0:T(8,128)} %f_hbm.1) | copy-start | bytes 221188
  2.6 0.7 %copy-start.2 = (bf16[1,4,2304]{2,1,0:T(4,128)(2,1)S(1)}, bf16[1,4,2304]{2,1,0:T(4,128)(2,1)}, u32[]{:S(2)}) copy-start(bf16[1,4,2304]{2,1,0:T(4,128)(2,1)} %q_hbm.1) | copy-start | bytes 55300

commit v2 on v1

--- a/solution.py
+++ b/solution.py
@@ -27,33 +27,51 @@
     )
 
 
+def split(x):
+    high = x.astype(jnp.bfloat16)
+    return high, (x - high.astype(jnp.float32)).astype(jnp.bfloat16)
+
+
 def precondition(query, factors, scale, modules, side):
     chunks = side // GROUP
     width = GROUP * side
     rows = modules * side
-    flat = jnp.concatenate([query[:, c * width : (c + 1) * width] for c in range(chunks)], axis=0)
-    spread = zero_one(
-        iota((rows, chunks * modules), 1)
-        == (iota((rows, chunks * modules), 0) % side) // GROUP * modules + iota((rows, chunks * modules), 0) // side
-    )
     keep = iota((rows, width), 0) % GROUP == iota((rows, width), 1) // side
-    fold = zero_one(iota((width, side), 0) % side == iota((width, side), 1))
-    matrices = dot(spread, flat.astype(jnp.bfloat16), (1, 0))
-    matrices = jnp.where(keep, matrices, 0.0).astype(jnp.bfloat16)
-    matrices = dot(matrices, fold, (1, 0))
-    outs = []
-    for m in range(modules):
-        left = dot(factors[m, 0], matrices[m * side : (m + 1) * side], (1, 0), HIGHEST)
-        outs.append(dot(left, factors[m, 1], (1, 0), HIGHEST))
-    both = (jnp.concatenate(outs, axis=0) / scale).astype(jnp.bfloat16)
-    wide = dot(both, fold, (1, 1))
-    wide = jnp.where(keep, wide, 0.0).astype(jnp.bfloat16)
-    return dot(spread, wide, (0, 0))
+    fold = zero_one(iota((width, rows), 0) % side == iota((width, rows), 1) % side)
+    tile = zero_one(iota((side, width), 0) == iota((side, width), 1) % side)
+    gather = zero_one(
+        iota((chunks * modules, rows), 0)
+        == (iota((chunks * modules, rows), 1) % side) // GROUP * modules + iota((chunks * modules, rows), 1) // side
+    )
+    block = iota((rows, rows), 0) // side == iota((rows, rows), 1) // side
+
+    spread = [
+        jnp.broadcast_to(query[m : m + 1, c * width : (c + 1) * width], (GROUP, width))
+        for m in range(modules)
+        for c in range(chunks)
+    ]
+    spread = jnp.where(keep, jnp.concatenate(spread, axis=0), 0.0).astype(jnp.bfloat16)
+    matrices = dot(spread, fold, (1, 0)).astype(jnp.bfloat16)
+
+    lefts = jnp.concatenate([factors[m, 0] for m in range(modules)], axis=0)
+    lefts = jnp.where(block, jnp.concatenate([lefts] * modules, axis=1), 0.0)
+    left_high, left_low = split(lefts)
+    left = dot(left_high, matrices, (1, 0)) + dot(left_low, matrices, (1, 0))
+    left = jnp.where(block, left, 0.0)
+    high, low = split(left)
+
+    rights = jnp.concatenate([factors[m, 1] for m in range(modules)], axis=0)
+    right_high, right_low = split(rights)
+    right_high = dot(right_high, tile, (1, 0)).astype(jnp.bfloat16)
+    right_low = dot(right_low, tile, (1, 0)).astype(jnp.bfloat16)
+    both = dot(high, right_high, (1, 0)) + (dot(low, right_high, (1, 0)) + dot(high, right_low, (1, 0)))
+    both = jnp.where(keep, both * (1.0 / scale), 0.0).astype(jnp.bfloat16)
+    return dot(gather, both, (1, 0))
 
 
 def kernel(
     rows_n, grp_scale, q_hbm, t_hbm, f_hbm, out_ref,
-    q_v, f_v, t_v, own, held, part, other,
+    q_v, f_v, t_v, own, held, part, other, pairs,
     in_sem, t_sem, send_sem, recv_sem, ex_sem,
 ):
     modules, coords = q_hbm.shape[1:]
@@ -117,17 +135,23 @@
     for step in range(1, rows_n):
         arrival(step).wait_recv()
 
-    total = jnp.zeros((train * modules, rows_n * modules), jnp.float32)
-    for j in range(tiles):
-        a = t_v[j].reshape(train * modules, LANES)
-        b = held[:, j].reshape(rows_n * modules, LANES)
-        total += dot(a, b, (1, 1))
-    same = iota(total.shape, 0) % modules == iota(total.shape, 1) % modules
-    total = jnp.where(same, total, 0.0)
-    pick_n = jnp.where(iota((train * modules, train), 0) // modules == iota((train * modules, train), 1), 1.0, 0.0)
-    pick_q = jnp.where(iota((rows_n, rows_n * modules), 1) // modules == iota((rows_n, rows_n * modules), 0), 1.0, 0.0)
-    by_n = dot(pick_n, total, (0, 0), HIGHEST)
-    scores = dot(pick_q, by_n, (1, 1), HIGHEST)
+    total = jnp.zeros((rows_n * modules, train * modules), jnp.float32)
+    a = jnp.concatenate([t_v[j].reshape(train * modules, LANES) for j in range(tiles)], axis=1)
+    b = jnp.concatenate([held[:, j].reshape(rows_n * modules, LANES) for j in range(tiles)], axis=1)
+    total = dot(b, a, (1, 1))
+    for k in range(train * modules // LANES):
+        pairs[k] = total[:, k * LANES : (k + 1) * LANES]
+    shape = (rows_n, train * modules)
+    which = iota(shape, 1) % modules
+    kept = jnp.zeros(shape, jnp.float32)
+    for m in range(modules):
+        some = [pairs[k, pl.ds(m, rows_n, stride=modules), :] for k in range(train * modules // LANES)]
+        kept = jnp.where(which == m, jnp.concatenate(some, axis=1), kept)
+    pick = zero_one(iota((train * modules, train), 0) // modules == iota((train * modules, train), 1))
+    high, low = split(kept)
+    low2 = (kept - high.astype(jnp.float32) - low.astype(jnp.float32)).astype(jnp.bfloat16)
+    summed = dot(jnp.concatenate([high, low, low2], axis=0), pick, (1, 0))
+    scores = summed[:rows_n] + (summed[rows_n : 2 * rows_n] + summed[2 * rows_n :])
     half = rows_n // 2
     part[0] = scores[:half]
     part[1] = scores[half:]
@@ -155,8 +179,8 @@
     half = rows_n // 2
     return pl.pallas_call(
         functools.partial(kernel, rows_n, scale),
-        out_shape=jax.ShapeDtypeStruct((half, train), jnp.float32),
-        in_specs=[pl.BlockSpec(memory_space=pl.ANY)] * 3,
+        out_shape=pltpu.VMEM((half, train), jnp.float32),
+        in_specs=[pl.BlockSpec(memory_space=pltpu.HBM)] * 3,
         out_specs=pl.BlockSpec(memory_space=pltpu.VMEM),
         scratch_shapes=[
             pltpu.VMEM(queries.shape, jnp.bfloat16),
@@ -166,6 +190,7 @@
             pltpu.VMEM((rows_n, tiles, modules, LANES), jnp.bfloat16),
             pltpu.VMEM((2, half, train), jnp.float32),
             pltpu.VMEM((half, train), jnp.float32),
+            pltpu.VMEM((train * modules // LANES, rows_n * modules, LANES), jnp.float32),
             pltpu.SemaphoreType.DMA((2,)),
             pltpu.SemaphoreType.DMA((tiles,)),
             pltpu.SemaphoreType.DMA((rows_n,)),
@@ -173,7 +198,7 @@
             pltpu.SemaphoreType.DMA((2,)),
         ],
         compiler_params=pltpu.CompilerParams(
-            collective_id=0, has_side_effects=True, vmem_limit_bytes=32 * 1024 * 1024
+            collective_id=0, has_side_effects=True, vmem_limit_bytes=60 * 1024 * 1024
         ),
     )(queries, train_grads, factors)
 

time: 17.3 us -> 12.7 us (0.73)
  local copies, waits for them, and re-layouts: 3.89 us -> 0.58 us
  Pallas kernels: 13.2 us -> 11.9 us
    unnamed x7 -> x1, local copies, waits for them, and re-layouts: 3.89 us -> 0.58 us
    pallas_call x1, Pallas kernels: 13.2 us -> 11.9 us  [shards(): pl.pallas_call(functools.partial(kernel, rows_n, scale), out_shape=pltpu....]
where the time goes in v2:
time: 12.7 us; the launch traced here: 12.5 us
  Pallas kernels  11.9 us (94%)
  local copies, waits for them, and re-layouts  0.58 us (5%)
    pallas_call x1, Pallas kernels, shards(): pl.pallas_call(functools.partial(kernel, rows_n, scale), out_shape=pltpu....  11.9 us
    unnamed x1, local copies, waits for them, and re-layouts  0.58 us

profile of v2, /device:TPU:0, one launch (start us, length us, event | category | flops | bytes accessed | tf_op | source)
XLA Modules:
  0.0 12.5 jit_solution(12987989141564673807)
XLA Ops:
  0.0 11.9 %shard_map.37 = f32[4,128]{1,0:T(4,128)S(1)} custom-call(bf16[1,4,2304]{2,1,0:T(4,128)(2,1)} %q_hbm.1, bf16[128,4,2304]{2,1,0:T(4,128)(2,1)} %t_hbm.1, f32[4,2,48,48]{3,2,1,0:T(8,128)} %f_hbm.1), custom_call_target="tpu_custom_call" | custom-call | tf_op jit(solution)/shard_map/pallas_call | solution.py:180
  12.0 0.6 %copy.5 = f32[4,128]{1,0:T(4,128)} copy(f32[4,128]{1,0:T(4,128)S(1)} %shard_map.37) | data formatting | bytes 4096

commit v3 on v2

--- a/solution.py
+++ b/solution.py
@@ -32,7 +32,7 @@
     return high, (x - high.astype(jnp.float32)).astype(jnp.bfloat16)
 
 
-def precondition(query, factors, scale, modules, side):
+def precondition(query, factors, scale, modules, side, f_copy):
     chunks = side // GROUP
     width = GROUP * side
     rows = modules * side
@@ -53,6 +53,7 @@
     spread = jnp.where(keep, jnp.concatenate(spread, axis=0), 0.0).astype(jnp.bfloat16)
     matrices = dot(spread, fold, (1, 0)).astype(jnp.bfloat16)
 
+    f_copy.wait()
     lefts = jnp.concatenate([factors[m, 0] for m in range(modules)], axis=0)
     lefts = jnp.where(block, jnp.concatenate([lefts] * modules, axis=1), 0.0)
     left_high, left_low = split(lefts)
@@ -71,7 +72,7 @@
 
 def kernel(
     rows_n, grp_scale, q_hbm, t_hbm, f_hbm, out_ref,
-    q_v, f_v, t_v, own, held, part, other, pairs,
+    q_v, f_v, t_v, own, held, part, other, pairs, train_v,
     in_sem, t_sem, send_sem, recv_sem, ex_sem,
 ):
     modules, coords = q_hbm.shape[1:]
@@ -94,12 +95,9 @@
     t_copies = [
         pltpu.make_async_copy(t_hbm.at[:, :, pl.ds(j * LANES, LANES)], t_v.at[j], t_sem.at[j]) for j in range(tiles)
     ]
-    for copy in t_copies:
-        copy.start()
 
     q_copy.wait()
-    f_copy.wait()
-    scaled = precondition(q_v[0].astype(jnp.float32), f_v, grp_scale, modules, side)
+    scaled = precondition(q_v[0].astype(jnp.float32), f_v, grp_scale, modules, side, f_copy)
     per = GROUP * side // LANES
     for j in range(tiles):
         c, t = divmod(j, per)
@@ -108,37 +106,46 @@
 
     pl.semaphore_wait(barrier, rows_n)
 
+    def target(step):
+        down, up = rows_n - step, step - 1
+        down = jnp.where(down > me, down, down - 1)
+        up = jnp.where(up < me, up, up + 1)
+        return jnp.where(2 * me < rows_n, down, up)
+
     def push(step):
         return pltpu.make_async_remote_copy(
             src_ref=own,
             dst_ref=held.at[me],
             send_sem=send_sem.at[step],
-            recv_sem=recv_sem.at[step],
-            device_id={"rows": lax.rem(me + step, rows_n)},
+            recv_sem=recv_sem.at[me],
+            device_id={"rows": target(step)},
         )
 
     def arrival(step):
-        source = lax.rem(me + rows_n - step, rows_n)
+        source = lax.rem(me + step, rows_n)
         return pltpu.make_async_remote_copy(
             src_ref=own,
             dst_ref=held.at[source],
             send_sem=send_sem.at[step],
-            recv_sem=recv_sem.at[step],
-            device_id={"rows": lax.rem(me + step, rows_n)},
+            recv_sem=recv_sem.at[source],
+            device_id={"rows": source},
         )
 
     for step in range(1, rows_n):
         push(step).start()
+    for copy in t_copies:
+        copy.start()
     held[me] = own[...]
     for copy in t_copies:
         copy.wait()
+    for j in range(tiles):
+        train_v[:, j * LANES : (j + 1) * LANES] = t_v[j].reshape(train * modules, LANES)
     for step in range(1, rows_n):
         arrival(step).wait_recv()
 
     total = jnp.zeros((rows_n * modules, train * modules), jnp.float32)
-    a = jnp.concatenate([t_v[j].reshape(train * modules, LANES) for j in range(tiles)], axis=1)
     b = jnp.concatenate([held[:, j].reshape(rows_n * modules, LANES) for j in range(tiles)], axis=1)
-    total = dot(b, a, (1, 1))
+    total = dot(b, train_v[...], (1, 1))
     for k in range(train * modules // LANES):
         pairs[k] = total[:, k * LANES : (k + 1) * LANES]
     shape = (rows_n, train * modules)
@@ -149,9 +156,8 @@
         kept = jnp.where(which == m, jnp.concatenate(some, axis=1), kept)
     pick = zero_one(iota((train * modules, train), 0) // modules == iota((train * modules, train), 1))
     high, low = split(kept)
-    low2 = (kept - high.astype(jnp.float32) - low.astype(jnp.float32)).astype(jnp.bfloat16)
-    summed = dot(jnp.concatenate([high, low, low2], axis=0), pick, (1, 0))
-    scores = summed[:rows_n] + (summed[rows_n : 2 * rows_n] + summed[2 * rows_n :])
+    summed = dot(jnp.concatenate([high, low], axis=0), pick, (1, 0))
+    scores = summed[:rows_n] + summed[rows_n:]
     half = rows_n // 2
     part[0] = scores[:half]
     part[1] = scores[half:]
@@ -191,6 +197,7 @@
             pltpu.VMEM((2, half, train), jnp.float32),
             pltpu.VMEM((half, train), jnp.float32),
             pltpu.VMEM((train * modules // LANES, rows_n * modules, LANES), jnp.float32),
+            pltpu.VMEM((train * modules, coords), jnp.bfloat16),
             pltpu.SemaphoreType.DMA((2,)),
             pltpu.SemaphoreType.DMA((tiles,)),
             pltpu.SemaphoreType.DMA((rows_n,)),

time: 12.7 us -> 12.6 us (level)
    pallas_call x1, Pallas kernels: 11.9 us -> 11.8 us  [shards(): pl.pallas_call(functools.partial(kernel, rows_n, scale), out_shape=pltpu....]
where the time goes in v3:
time: 12.6 us; the launch traced here: 12.4 us
  Pallas kernels  11.8 us (94%)
  local copies, waits for them, and re-layouts  0.58 us (5%)
    pallas_call x1, Pallas kernels, shards(): pl.pallas_call(functools.partial(kernel, rows_n, scale), out_shape=pltpu....  11.8 us
    unnamed x1, local copies, waits for them, and re-layouts  0.58 us

profile of v3, /device:TPU:0, one launch (start us, length us, event | category | flops | bytes accessed | tf_op | source)
XLA Modules:
  0.0 12.4 jit_solution(51350592577040424)
XLA Ops:
  0.0 11.8 %shard_map.37 = f32[4,128]{1,0:T(4,128)S(1)} custom-call(bf16[1,4,2304]{2,1,0:T(4,128)(2,1)} %q_hbm.1, bf16[128,4,2304]{2,1,0:T(4,128)(2,1)} %t_hbm.1, f32[4,2,48,48]{3,2,1,0:T(8,128)} %f_hbm.1), custom_call_target="tpu_custom_call" | custom-call | tf_op jit(solution)/shard_map/pallas_call | solution.py:186
  11.8 0.6 %copy.5 = f32[4,128]{1,0:T(4,128)} copy(f32[4,128]{1,0:T(4,128)S(1)} %shard_map.37) | data formatting | bytes 4096

commit v4 on v3

--- a/solution.py
+++ b/solution.py
@@ -57,7 +57,8 @@
     lefts = jnp.concatenate([factors[m, 0] for m in range(modules)], axis=0)
     lefts = jnp.where(block, jnp.concatenate([lefts] * modules, axis=1), 0.0)
     left_high, left_low = split(lefts)
-    left = dot(left_high, matrices, (1, 0)) + dot(left_low, matrices, (1, 0))
+    left = dot(jnp.concatenate([left_high, left_low], axis=0), matrices, (1, 0))
+    left = left[:rows] + left[rows:]
     left = jnp.where(block, left, 0.0)
     high, low = split(left)
 
@@ -65,7 +66,8 @@
     right_high, right_low = split(rights)
     right_high = dot(right_high, tile, (1, 0)).astype(jnp.bfloat16)
     right_low = dot(right_low, tile, (1, 0)).astype(jnp.bfloat16)
-    both = dot(high, right_high, (1, 0)) + (dot(low, right_high, (1, 0)) + dot(high, right_low, (1, 0)))
+    stacked = dot(jnp.concatenate([high, low], axis=0), right_high, (1, 0))
+    both = stacked[:rows] + (stacked[rows:] + dot(high, right_low, (1, 0)))
     both = jnp.where(keep, both * (1.0 / scale), 0.0).astype(jnp.bfloat16)
     return dot(gather, both, (1, 0))
 

time: 12.6 us -> 12.5 us (level)
  no operation moved by 1% of the time
where the time goes in v4:
time: 12.5 us; the launch traced here: 12.4 us
  Pallas kernels  11.8 us (94%)
  local copies, waits for them, and re-layouts  0.58 us (5%)
    pallas_call x1, Pallas kernels, shards(): pl.pallas_call(functools.partial(kernel, rows_n, scale), out_shape=pltpu....  11.8 us
    unnamed x1, local copies, waits for them, and re-layouts  0.58 us

profile of v4, /device:TPU:0, one launch (start us, length us, event | category | flops | bytes accessed | tf_op | source)
XLA Modules:
  0.0 12.4 jit_solution(4496163123714460653)
XLA Ops:
  0.0 11.8 %shard_map.37 = f32[4,128]{1,0:T(4,128)S(1)} custom-call(bf16[1,4,2304]{2,1,0:T(4,128)(2,1)} %q_hbm.1, bf16[128,4,2304]{2,1,0:T(4,128)(2,1)} %t_hbm.1, f32[4,2,48,48]{3,2,1,0:T(8,128)} %f_hbm.1), custom_call_target="tpu_custom_call" | custom-call | tf_op jit(solution)/shard_map/pallas_call | solution.py:188
  11.8 0.6 %copy.5 = f32[4,128]{1,0:T(4,128)} copy(f32[4,128]{1,0:T(4,128)S(1)} %shard_map.37) | data formatting | bytes 4096
